TPU v7x, 128 devices: a whole 4x4x4 slice. The times are simulated.
128 devices in a mesh: chan: 8 (over z, y_lo), win: 16 (over y_hi, x, core).
Axes of the slice: x: 4, y: 4 (y_hi: 2, y_lo: 2; y = y_hi * 2 + y_lo), z: 4, core: 2. Of those that a mesh axis runs over, the one named last changes fastest.
Arguments:
- raw_traces: bfloat16 [32, 2048, 4096], P('win', None, 'chan'), may hold values from -6 to 6
- fir_taps: bfloat16 [32], replicated, may hold values from -1 to 1
- source_ids: int32 [4], replicated, may hold values from 0 to 15
- window_offsets: int32 [32], P('win'), may hold values from 0 to 3
Outputs:
- correlations: float32 [16384, 2048], P('win', 'chan')
All inputs are finite; a program needn't handle non-finite values.
Results may differ from a plain program's by a relative error of at most 0.008.
Values may be sent and summed in bfloat16 or wider, within the bound.
No kernel may reach another device: no remote copies, remote signals or barrier semaphores. Data moves between devices by JAX's collectives and lax.ppermute only.
A program may use at most 192 MiB of HBM per device.

v0:
```python
import math

import jax
import jax.numpy as jnp
from jax import lax
from jax.sharding import PartitionSpec as P

BLOCK = 128
DECIM = 4
BAND = 64
NSRC = 4
LAGS = 32


epsilon = 1e-06
clip_level = 2.0


def spread(x, axis, root):
    mine = lax.axis_index(axis) == root
    return lax.psum(jnp.where(mine, x, jnp.zeros_like(x)), axis)


def band_matrix(distance, tap_values):
    tap_ids = jnp.arange(tap_values.shape[0], dtype=jnp.int32)
    onehot = (distance[..., None] == tap_ids).astype(jnp.float32)
    return jnp.einsum("wtmk,k->wtm", onehot, tap_values.astype(jnp.float32)).astype(jnp.bfloat16)


def decimate(normed, tap_values, offsets):
    windows_here, channels_here, samples = normed.shape
    tile_len = 512
    tile_count = samples // tile_len
    out_width = tile_len // DECIM
    tile_pos = jnp.arange(tile_len, dtype=jnp.int32)[:, None]
    out_pos = jnp.arange(out_width, dtype=jnp.int32)[None, :]
    distance = (DECIM * out_pos - tile_pos)[None] + offsets[:, None, None]
    own_matrix = band_matrix(distance, tap_values)
    prior_matrix = band_matrix(distance + tile_len, tap_values)
    tiles = normed.reshape(windows_here, channels_here, tile_count, tile_len)
    prior_tiles = jnp.concatenate([jnp.zeros_like(tiles[:, :, :1]), tiles[:, :, :-1]], axis=2)
    result = jnp.einsum("wcbt,wtm->wcbm", tiles, own_matrix, preferred_element_type=jnp.float32)
    result = result + jnp.einsum(
        "wcbt,wtm->wcbm", prior_tiles, prior_matrix, preferred_element_type=jnp.float32
    )
    return result.reshape(windows_here, channels_here, tile_count * out_width).astype(jnp.bfloat16)


def transform_table(length):
    freq_count = length // 2
    sample_ids = jnp.arange(length, dtype=jnp.int32)[:, None]
    freq_ids = jnp.arange(freq_count, dtype=jnp.int32)[None, :]
    angles = (sample_ids * freq_ids % length).astype(jnp.float32) * (2.0 * math.pi / length)
    return jnp.concatenate([jnp.cos(angles), -jnp.sin(angles)], axis=1).astype(jnp.bfloat16)


def whiten_spectra(decimated):
    windows_here, channels_here, length = decimated.shape
    cos_sin = transform_table(length)
    transform = jnp.dot(
        decimated.reshape(windows_here * channels_here, length),
        cos_sin,
        preferred_element_type=jnp.float32,
    )
    freq_count = length // 2
    halves = transform.reshape(windows_here, channels_here, 2, freq_count // BAND, BAND)
    energy = jnp.mean(
        halves[:, :, 0] * halves[:, :, 0] + halves[:, :, 1] * halves[:, :, 1],
        axis=-1,
        keepdims=True,
    )
    whitened = halves / jnp.sqrt(energy + epsilon)[:, :, None]
    return whitened.reshape(windows_here, channels_here, length).astype(jnp.bfloat16)


def modulate(source_rows, lag_count):
    window_count, row_count, length = source_rows.shape
    freq_count = length // 2
    lag_ids = jnp.arange(1, lag_count + 1, dtype=jnp.int32)[:, None]
    freq_ids = jnp.arange(freq_count, dtype=jnp.int32)[None, :]
    angles = (lag_ids * freq_ids % length).astype(jnp.float32) * (2.0 * math.pi / length)
    cos_part = jnp.cos(angles)
    sin_part = jnp.sin(angles)
    real_part = source_rows[..., :freq_count].astype(jnp.float32)[:, :, None, :]
    imag_part = source_rows[..., freq_count:].astype(jnp.float32)[:, :, None, :]
    mod_real = real_part * cos_part - imag_part * sin_part
    mod_imag = real_part * sin_part + imag_part * cos_part
    joined = jnp.concatenate([mod_real, mod_imag], axis=-1).astype(jnp.bfloat16)
    return joined.reshape(window_count, row_count * lag_count, length)


def contract(modulated, receivers):
    return lax.dot_general(
        modulated, receivers, (((0, 2), (0, 2)), ((), ())), preferred_element_type=jnp.float32
    )


def on_device(raw_traces, fir_taps, source_ids, window_offsets):
    regrouped = lax.all_to_all(raw_traces, "chan", split_axis=1, concat_axis=2, tiled=True)
    values = regrouped.astype(jnp.float32)
    mean_square = jnp.mean(values * values, axis=-1, keepdims=True)
    normed = jnp.clip(values / jnp.sqrt(mean_square + epsilon), -clip_level, clip_level).astype(
        jnp.bfloat16
    )
    decimated = decimate(normed, fir_taps, window_offsets)
    spectra = whiten_spectra(decimated)
    local_windows, local_channels, length = spectra.shape
    blocks_here = local_channels // BLOCK
    gathered_blocks = []
    for source_step in range(NSRC):
        block_id = source_ids[source_step]
        chosen = lax.dynamic_slice_in_dim(spectra, block_id % blocks_here * BLOCK, BLOCK, 1)
        gathered_blocks.append(spread(chosen, "chan", block_id // blocks_here))
    sources = jnp.concatenate(gathered_blocks, axis=1)
    windows_all = local_windows * lax.axis_size("win")
    own_sources = lax.all_to_all(sources, "win", split_axis=1, concat_axis=0, tiled=True)
    total = contract(
        modulate(own_sources, LAGS), lax.all_gather(spectra, "win", axis=0, tiled=True)
    )
    return total / math.sqrt(length // 2 * windows_all)


def solution(mesh):
    placed = (P("win", None, "chan"), P(), P(), P("win"))
    return jax.shard_map(
        on_device, mesh=mesh, in_specs=placed, out_specs=P("win", "chan"), check_vma=False
    )
```

profile of v0, /device:TPU:1, one launch (start us, length us, event | category | flops | bytes accessed | tf_op | source)
XLA Modules:
  0.0 367.7 jit_solution(6348188632731301300)
XLA Ops:
  7.4 10.1 %copy.44 = bf16[2,2048,512]{2,0,1:T(2,128)(2,1)} copy(bf16[2,2048,512]{2,1,0:T(8,128)(2,1)} %param.4) | data formatting | bytes 8388608 | tf_op args[0]
  17.5 7.0 %all-to-all-start = ((bf16[2,2048,512]{2,0,1:T(2,128)(2,1)}), bf16[2,2048,512]{2,0,1:T(2,128)(2,1)}, u32[]{:S(2)}, u32[]{:S(2)}) async-start(bf16[2,2048,512]{2,0,1:T(2,128)(2,1)} %copy.44), calls=%async_computation | async-start | bytes 8388608 | tf_op jit(solution)/shard_map/all_to_all | solution.py:99
  24.5 0.0 all-reduce.4.cloned.1.call-start
  24.6 0.6 fusion.50
  34.9 0.0 copy-done.3
  34.9 0.1 broadcast_add_fusion
  35.0 2.7 fusion.8
  37.7 0.5 copy.55
  38.2 2.7 fusion.9
  40.9 0.3 copy.58
  41.4 8.5 %negate_convert_fusion = (bf16[1024,512]{0,1:T(8,128)(2,1)S(1)}, bf16[1024,512]{0,1:T(8,128)(2,1)S(1)}) fusion(), kind=kLoop, calls=%fused_computation.35 | loop fusion | flops 8912896 | bytes 2097152 | tf_op jit(solution)/shard_map/convert.4
  49.9 0.2 pad_maximum_fusion
  50.1 23.1 %all-to-all-done = bf16[2,2048,512]{2,0,1:T(2,128)(2,1)} async-done(((bf16[2,2048,512]{2,0,1:T(2,128)(2,1)}), bf16[2,2048,512]{2,0,1:T(2,128)(2,1)}, u32[]{:S(2)}, u32[]{:S(2)}) %all-to-all-start) | async-done | bytes 4194336 | tf_op jit(solution)/shard_map/all_to_all | solution.py:99
  73.2 2.9 copy.45
  76.0 0.9 fusion.10
  76.9 3.4 fusion.15
  80.3 1.5 fusion.35
  81.8 1.2 add_convert_fusion
  83.0 1.3 fusion.51
  84.2 0.2 fusion.33
  84.4 0.3 divide_convert_fusion
  84.7 1.2 constant_dynamic-slice_fusion.3
  85.9 0.5 copy.66
  86.4 0.5 copy.65
  86.9 0.5 copy.64
  87.4 1.6 copy.63
  89.1 1.2 broadcast_select_fusion
  90.3 1.2 broadcast_select_fusion.1
  91.5 1.3 broadcast_select_fusion.2
  92.8 1.2 broadcast_select_fusion.3
  94.0 0.0 all-reduce.4.cloned.1.call-update
  94.0 0.0 all-gather.2.cloned.1.call-start
  94.1 1.3 copy.53
  95.4 0.0 all-gather.2.cloned.1.call-update
  95.4 162.4 %all-reduce.4.cloned.1.call-done = (bf16[2,128,1024]{2,0,1:T(2,128)(2,1)}, bf16[2,128,1024]{2,0,1:T(2,128)(2,1)}, bf16[2,128,1024]{2,0,1:T(2,128)(2,1)}, bf16[2,128,1024]{2,0,1:T(2,128)(2,1)}) async-done(((bf16[2,128,1024]{2,0,1:T(2,128)(2,1)}, bf16[2,128,1024]{2,0,1:T(2,128)(2,1)}, bf16[2,128,1024]{2,0,1:T(2,128)(2,1)}, bf16[2,128,1024]{2,0,1:T(2,128)(2,1)}), (bf16[2,128,1024]{2,0,1:T(2,128)(2,1)}, ...) | async-done | bytes 2097168 | tf_op jit(solution)/shard_map/psum | solution.py:21
  257.8 5.5 %pad_maximum_fusion.1 = bf16[2,512,1024]{2,0,1:T(2,128)(2,1)} fusion(bf16[2,128,1024]{2,0,1:T(2,128)(2,1)} %get-tuple-element.5, bf16[2,128,1024]{2,0,1:T(2,128)(2,1)} %get-tuple-element.6, bf16[2,128,1024]{2,0,1:T(2,128)(2,1)} %get-tuple-element.7, bf16[2,128,1024]{2,0,1:T(2,128)(2,1)} %get-tuple-element.8), kind=kLoop, calls=%fused_computation.33 | loop fusion | flops 3145728 | bytes 4194304 | tf_op jit(solution)/shard_map/concatenate | solution.py:114
  263.3 7.2 %all-to-all-start.1 = ((bf16[2,512,1024]{2,0,1:T(2,128)(2,1)}), bf16[2,512,1024]{2,0,1:T(2,128)(2,1)S(1)}, u32[]{:S(2)}, u32[]{:S(2)}) async-start(bf16[2,512,1024]{2,0,1:T(2,128)(2,1)} %pad_maximum_fusion.1), calls=%async_computation.1 | async-start | bytes 4194304 | tf_op jit(solution)/shard_map/all_to_all | solution.py:116
  270.6 0.3 fusion.46
  270.9 28.2 %all-to-all-done.1 = bf16[2,512,1024]{2,0,1:T(2,128)(2,1)S(1)} async-done(((bf16[2,512,1024]{2,0,1:T(2,128)(2,1)}), bf16[2,512,1024]{2,0,1:T(2,128)(2,1)S(1)}, u32[]{:S(2)}, u32[]{:S(2)}) %all-to-all-start.1) | async-done | bytes 2097184 | tf_op jit(solution)/shard_map/all_to_all | solution.py:116
  299.2 0.6 copy.51
  299.8 0.3 copy.52
  300.0 1.9 slice_convert_fusion.1
  302.0 1.6 mul.213
  303.6 1.6 mul.219
  305.2 24.8 %fusion.1 = (bf16[32,1024,512]{2,1,0:T(8,128)(2,1)}, bf16[32,1024,512]{2,1,0:T(8,128)(2,1)}) fusion(f32[1024,512]{1,0:T(8,128)} %bitcast.85, f32[32,32,512]{2,1,0:T(8,128)} %get-tuple-element.12, f32[1024,512]{1,0:T(8,128)} %bitcast.84, f32[32,32,512]{2,1,0:T(8,128)S(1)} %get-tuple-element.11), kind=kLoop, calls=%fused_computation.5 | loop fusion | flops 134217728 | bytes 75497472 | tf_op jit(solution)/shard_map/convert.1
  330.0 0.0 all-gather.2.cloned.1.call-done
  330.0 0.0 copy-start.1
  330.0 30.2 %fusion.29 = f32[1024,256]{1,0:T(8,128)} fusion(bf16[32,256,1024]{2,1,0:T(8,128)(2,1)} %all-gather.2.cloned.1.call-done, bf16[32,1024,512]{2,1,0:T(8,128)(2,1)} %get-tuple-element.10, bf16[32,1024,512]{2,1,0:T(8,128)(2,1)} %get-tuple-element.9), kind=kOutput, calls=%fused_computation.42 | convolution fusion | flops 17314349056 | bytes 84934656 | tf_op jit(solution)/shard_map/dot_general | solution.py:93
  (11 shorter events, 0.1 us)
Async XLA Ops:
  7.4 27.6 %copy-start = (bf16[32]{0:T(256)(128)(2,1)S(1)}, bf16[32]{0:T(256)(128)(2,1)}, u32[]{:S(2)}) copy-start(bf16[32]{0:T(256)(128)(2,1)} %param.5) | copy-start | bytes 196
  17.5 7.1 %copy-start.2 = (s32[4]{0:T(128)S(1)}, s32[4]{0:T(128)}, u32[]{:S(2)}) copy-start(s32[4]{0:T(128)} %param.6) | copy-start | bytes 52
  17.5 17.4 %copy-start.3 = (s32[2]{0:T(128)S(1)}, s32[2]{0:T(128)}, u32[]{:S(2)}) copy-start(s32[2]{0:T(128)} %param.7) | copy-start | bytes 28
  17.5 55.7 %all-to-all-start = ((bf16[2,2048,512]{2,0,1:T(2,128)(2,1)}), bf16[2,2048,512]{2,0,1:T(2,128)(2,1)}, u32[]{:S(2)}, u32[]{:S(2)}) async-start(bf16[2,2048,512]{2,0,1:T(2,128)(2,1)} %copy.44), calls=%async_computation | async-start | bytes 8388608 | tf_op jit(solution)/shard_map/all_to_all | solution.py:99
  24.5 233.3 %all-reduce.4.cloned.1.call-start = ((), (), s32[]{:S(2)}) async-start(), calls=%async_computation.3 | async-start | bytes 4194304 | tf_op jit(solution)/shard_map/psum | solution.py:21
  94.0 236.0 %all-gather.2.cloned.1.call-start = ((), (), s32[]{:S(2)}) async-start(), calls=%async_computation.2 | async-start | bytes 17825792 | tf_op jit(solution)/shard_map/all_gather | solution.py:118
  263.3 35.8 %all-to-all-start.1 = ((bf16[2,512,1024]{2,0,1:T(2,128)(2,1)}), bf16[2,512,1024]{2,0,1:T(2,128)(2,1)S(1)}, u32[]{:S(2)}, u32[]{:S(2)}) async-start(bf16[2,512,1024]{2,0,1:T(2,128)(2,1)} %pad_maximum_fusion.1), calls=%async_computation.1 | async-start | bytes 4194304 | tf_op jit(solution)/shard_map/all_to_all | solution.py:116
  330.0 30.2 %copy-start.1 = (bf16[32]{0:T(256)(128)(2,1)S(1)}, bf16[32]{0:T(256)(128)(2,1)}, u32[]{:S(2)}) copy-start(bf16[32]{0:T(256)(128)(2,1)} %param.5) | copy-start | bytes 196
Sparse Core Ops, SparseCore 0:
  94.1 163.6 all-reduce.3
Sparse Core Ops, SparseCore 1:
  96.9 115.6 all-gather.1
where the time goes:
time: 368 us
  waiting for transfers between devices  214 us (58%)
  other arithmetic  51.1 us (14%)
  matrix products  39.5 us (11%)
  between operations  24.8 us (7%)
  local copies, waits for them, and re-layouts  24.2 us (7%)
  starting transfers between devices  14.3 us (4%)
    psum x1, waiting for transfers between devices, spread(): return lax.psum(jnp.where(mine, x, jnp.zeros_like(x)), axis)  162 us
    another operation x2, other arithmetic  33.3 us
    dot_general x1, matrix products, contract(): lax.dot_general(modulated, receivers, (((0, 2), (0, 2)), ((), ())), prefe...  30.2 us
    all_to_all x1, waiting for transfers between devices, on_device(): lax.all_to_all(sources, 'win', split_axis=1, concat_axis=0, tiled=True)  28.2 us
    all_to_all x1, waiting for transfers between devices, on_device(): lax.all_to_all(raw_traces, 'chan', split_axis=1, concat_axis=2, tiled=True)  23.1 us
    unnamed x13, local copies, waits for them, and re-layouts  13.3 us
  transfers between devices with their start and end apart: 4, of which 3 were waited for; matrix products, arithmetic and copies ran while one was open for 15% of the time, Pallas kernels for 0%

commit v1 on v0

v1 whole, which is shorter than its diff:
```python
import functools
import math

import jax
import jax.numpy as jnp
import numpy as np
from jax import lax
from jax.experimental import pallas as pl
from jax.experimental.pallas import tpu as pltpu
from jax.sharding import PartitionSpec as P

SAMPLES = 4096
DECIM = 4
TAPS = 32
NSRC = 4
LENGTH = 1024
FREQS = 512
BAND = 64
NCHAN = 8
NPAIR = 8
FINE = 8
COARSE = 4
STAGES = 2
HERE = 512
OUT = HERE // DECIM
RECV = 256
PART = 32 // STAGES
ROWS = NPAIR * PART
VMEM = 56 * 1024 * 1024

epsilon = 1e-06
clip_level = 2.0

f32 = jnp.float32
bf16 = jnp.bfloat16

NT = (((1,), (1,)), ((), ()))
TN = (((0,), (0,)), ((), ()))


def dot(a, b, dims=None):
    if dims is None:
        return jnp.dot(a, b, preferred_element_type=f32)
    return lax.dot_general(a, b, dims, preferred_element_type=f32)


def split_dot(left, sq, dims, flip=False):
    hi = sq.astype(bf16)
    lo = (sq - hi.astype(f32)).astype(bf16)
    if flip:
        return dot(hi, left, dims) + dot(lo, left, dims)
    return dot(left, hi, dims) + dot(left, lo, dims)


def params(limit=VMEM):
    return pltpu.CompilerParams(vmem_limit_bytes=limit)


def cost(flops, nbytes):
    return pl.CostEstimate(flops=int(flops), bytes_accessed=int(nbytes), transcendentals=0)


@functools.lru_cache(None)
def tables():
    m = np.arange(LENGTH)[:, None]
    f = np.arange(FREQS)[None, :]
    ang = (m * f % LENGTH).astype(np.float64) * (2.0 * math.pi / LENGTH)
    table = np.concatenate([np.cos(ang), -np.sin(ang)], axis=1).astype(jnp.bfloat16)
    band = np.kron(np.eye(FREQS // BAND), np.ones((BAND, BAND))) / BAND
    lag = np.arange(1, FINE + 1)[:, None]
    fine = (lag * f % LENGTH) * (2.0 * math.pi / LENGTH)
    fine = np.concatenate([np.cos(fine), np.sin(fine)], axis=1).astype(np.float32)
    coarse = (FINE * np.arange(COARSE)[:, None] * f % LENGTH) * (2.0 * math.pi / LENGTH)
    coarse = np.stack([np.cos(coarse), np.sin(coarse)], axis=1).astype(np.float32)
    coarse = np.broadcast_to(coarse[..., None], (COARSE, 2, FREQS, 128)).copy()
    pick = np.zeros((TAPS, 128), np.float32)
    pick[np.arange(TAPS), 128 - TAPS + np.arange(TAPS)] = 1.0
    return table, np.ascontiguousarray(table.T), band.astype(jnp.bfloat16), fine, coarse, pick.astype(jnp.bfloat16)


def power_kernel(x_ref, pick_ref, s_ref, t_ref):
    ones = jnp.ones((NCHAN, HERE), bf16)
    for w in range(2):
        x = x_ref[w]
        xf = x.astype(f32)
        s_ref[:, w, :] = split_dot(ones, xf * xf, NT)
        t_ref[w] = dot(pick_ref[...], x[:, HERE - 128:], NT).astype(bf16)


def power_and_tail(raw, pick):
    step = 512
    channels = raw.shape[1]
    return pl.pallas_call(
        power_kernel,
        grid=(channels // step,),
        in_specs=[
            pl.BlockSpec((2, step, HERE), lambda i: (0, i, 0)),
            pl.BlockSpec((TAPS, 128), lambda i: (0, 0)),
        ],
        out_specs=[
            pl.BlockSpec((NCHAN, 2, step), lambda i: (0, 0, i)),
            pl.BlockSpec((2, TAPS, step), lambda i: (0, 0, i)),
        ],
        out_shape=[
            jax.ShapeDtypeStruct((NCHAN, 2, channels), f32),
            jax.ShapeDtypeStruct((2, TAPS, channels), bf16),
        ],
        compiler_params=params(),
        cost_estimate=cost(4e8, 5e6),
        name="power",
    )(raw, pick)


def bands(taps, offsets):
    pos = jnp.arange(-TAPS, HERE, dtype=jnp.int32)[:, None]
    out = jnp.arange(OUT, dtype=jnp.int32)[None, :]
    distance = (DECIM * out - pos)[None] + offsets[:, None, None]
    ids = jnp.arange(TAPS, dtype=jnp.int32)[:, None, None, None]
    full = jnp.sum(
        jnp.where(distance[None] == ids, taps.astype(f32)[:, None, None, None], 0.0), axis=0
    ).astype(bf16)
    return full[:, TAPS:], full[:, :TAPS]


def decimate_rows(x, sums, tail, own, prior):
    n = x.shape[0]
    inv = lax.rsqrt(jnp.sum(sums, axis=0, keepdims=True) * (1.0 / SAMPLES) + epsilon)
    cols = jnp.transpose(jnp.broadcast_to(inv, (128, n)))
    cols = jnp.concatenate([cols] * (HERE // 128), axis=1)
    normed = jnp.clip(x.astype(f32) * cols, -clip_level, clip_level).astype(bf16)
    tail_normed = jnp.clip(tail.astype(f32) * inv, -clip_level, clip_level).astype(bf16)
    return (dot(normed, own) + dot(tail_normed, prior, TN)).astype(bf16)


def receive_kernel(x_ref, s_ref, t_ref, own_ref, prior_ref, o_ref):
    for w in range(2):
        o_ref[0, w] = decimate_rows(x_ref[w], s_ref[:, w, :], t_ref[w], own_ref[w], prior_ref[w])


def decimate_receivers(raw, sums, tail, own, prior):
    return pl.pallas_call(
        receive_kernel,
        grid=(NCHAN,),
        in_specs=[
            pl.BlockSpec((2, RECV, HERE), lambda i: (0, i, 0)),
            pl.BlockSpec((NCHAN, 2, RECV), lambda i: (0, 0, i)),
            pl.BlockSpec((2, TAPS, RECV), lambda i: (0, 0, i)),
            pl.BlockSpec((2, HERE, OUT), lambda i: (0, 0, 0)),
            pl.BlockSpec((2, TAPS, OUT), lambda i: (0, 0, 0)),
        ],
        out_specs=pl.BlockSpec((1, 2, RECV, OUT), lambda i: (i, 0, 0, 0)),
        out_shape=jax.ShapeDtypeStruct((NCHAN, 2, RECV, OUT), bf16),
        compiler_params=params(),
        cost_estimate=cost(6e8, 6e6),
        name="decimate_receivers",
    )(raw, sums, tail, own, prior)


def source_kernel(ids_ref, core_ref, x_ref, s_ref, t_ref, own_ref, prior_ref, o_ref):
    first = core_ref[0] == 0
    for w in range(2):
        dec = decimate_rows(x_ref[w], s_ref[:, w, :], t_ref[w], own_ref[w], prior_ref[w])
        for t in range(2):
            for s in range(STAGES):
                low = 64 * t + PART * s
                even, odd = dec[low:low + PART], dec[low + 32:low + 32 + PART]
                o_ref[0, s, w, t] = jnp.where(first, even, odd)
                o_ref[1, s, w, t] = jnp.where(first, odd, even)


def decimate_sources(ids, core, raw, sums, tail, own, prior):
    return pl.pallas_call(
        source_kernel,
        grid_spec=pltpu.PrefetchScalarGridSpec(
            num_scalar_prefetch=2,
            grid=(NSRC,),
            in_specs=[
                pl.BlockSpec((2, 128, HERE), lambda q, ids, c: (0, ids[q], 0)),
                pl.BlockSpec((NCHAN, 2, 128), lambda q, ids, c: (0, 0, ids[q])),
                pl.BlockSpec((2, TAPS, 128), lambda q, ids, c: (0, 0, ids[q])),
                pl.BlockSpec((2, HERE, OUT), lambda q, ids, c: (0, 0, 0)),
                pl.BlockSpec((2, TAPS, OUT), lambda q, ids, c: (0, 0, 0)),
            ],
            out_specs=pl.BlockSpec(
                (2, STAGES, 2, 2, PART, OUT), lambda q, ids, c: (0, 0, 0, q, 0, 0)
            ),
        ),
        out_shape=jax.ShapeDtypeStruct((2, STAGES, 2, NPAIR, PART, OUT), bf16),
        compiler_params=params(),
        cost_estimate=cost(1.5e8, 2e6),
        name="decimate_sources",
    )(ids, core, raw, sums, tail, own, prior)


def receiver_kernel(x_ref, table_ref, o_ref):
    x = jnp.concatenate([x_ref[j, 0] for j in range(NCHAN)], axis=1)
    spec = dot(table_ref[...], x, NT)
    re, im = spec[:FREQS], spec[FREQS:]
    energy = jnp.mean((re * re + im * im).reshape(FREQS // BAND, BAND, RECV), axis=1, keepdims=True)
    gain = lax.rsqrt(energy + epsilon)
    halves = spec.reshape(2, FREQS // BAND, BAND, RECV) * gain[None]
    o_ref[0] = halves.reshape(LENGTH, RECV).astype(bf16)


def receiver_spectra(blocks, table_t):
    return pl.pallas_call(
        receiver_kernel,
        grid=(2,),
        in_specs=[
            pl.BlockSpec((NCHAN, 1, RECV, OUT), lambda w: (0, w, 0, 0)),
            pl.BlockSpec((LENGTH, LENGTH), lambda w: (0, 0)),
        ],
        out_specs=pl.BlockSpec((1, LENGTH, RECV), lambda w: (w, 0, 0)),
        out_shape=jax.ShapeDtypeStruct((2, LENGTH, RECV), bf16),
        compiler_params=params(),
        cost_estimate=cost(1.1e9, 4e6),
        name="receiver_spectra",
    )(blocks, table_t)


def shift_kernel(own_ref, mate_ref, twiddle_ref, o_ref):
    w = pl.program_id(0)
    for c in range(RECV // 128):
        lanes = pl.ds(c * 128, 128)
        spec = jnp.where(w < 2, own_ref[0, :, lanes], mate_ref[0, :, lanes])
        o_ref[:, lanes] = spec
        re, im = spec[:FREQS].astype(f32), spec[FREQS:].astype(f32)
        for a in range(1, COARSE):
            cos, sin = twiddle_ref[a, 0], twiddle_ref[a, 1]
            at = pl.ds(a * RECV + c * 128, 128)
            o_ref[:FREQS, at] = (re * cos + im * sin).astype(bf16)
            o_ref[FREQS:, at] = (im * cos - re * sin).astype(bf16)


def shifted_receivers(own, mate, twiddle):
    return pl.pallas_call(
        shift_kernel,
        grid=(4,),
        in_specs=[
            pl.BlockSpec((1, LENGTH, RECV), lambda w: (jnp.minimum(w, 1), 0, 0)),
            pl.BlockSpec((1, LENGTH, RECV), lambda w: (jnp.maximum(w - 2, 0), 0, 0)),
            pl.BlockSpec((COARSE, 2, FREQS, 128), lambda w: (0, 0, 0, 0)),
        ],
        out_specs=pl.BlockSpec((LENGTH, COARSE * RECV), lambda w: (w, 0)),
        out_shape=jax.ShapeDtypeStruct((4 * LENGTH, COARSE * RECV), bf16),
        compiler_params=params(),
        cost_estimate=cost(3e7, 1.2e7),
        name="shifted_receivers",
    )(own, mate, twiddle)


def correlate_kernel(x_ref, table_ref, band_ref, fine_ref, recv_ref, o_ref, acc_ref):
    w = pl.program_id(0)
    x = jnp.concatenate([x_ref[j, 0] for j in range(NCHAN)], axis=1)
    spec = dot(x, table_ref[...])
    re, im = spec[:, :FREQS], spec[:, FREQS:]
    energy = split_dot(band_ref[...], re * re + im * im, None, flip=True)
    gain = lax.rsqrt(energy + epsilon)
    re = (re * gain).astype(bf16).astype(f32)
    im = (im * gain).astype(bf16).astype(f32)
    cos, sin = fine_ref[:, :FREQS][None], fine_ref[:, FREQS:][None]
    for p in range(NPAIR):
        a = re[p * PART:(p + 1) * PART][:, None, :]
        b = im[p * PART:(p + 1) * PART][:, None, :]
        rows = PART * FINE
        left = jnp.concatenate(
            [
                (a * cos - b * sin).reshape(rows, FREQS).astype(bf16),
                (a * sin + b * cos).reshape(rows, FREQS).astype(bf16),
            ],
            axis=1,
        )
        part = dot(left, recv_ref[...])

        @pl.when(w == 0)
        def _():
            acc_ref[p] = part

        @pl.when((w > 0) & (w < 3))
        def _():
            acc_ref[p] += part

        @pl.when(w == 3)
        def _():
            o_ref[p] = (acc_ref[p] + part).astype(bf16)


def correlate(blocks, table, band, fine, recv):
    rows = PART * FINE
    return pl.pallas_call(
        correlate_kernel,
        grid=(4,),
        in_specs=[
            pl.BlockSpec((NCHAN, 1, ROWS, OUT), lambda w: (0, w, 0, 0)),
            pl.BlockSpec((LENGTH, LENGTH), lambda w: (0, 0)),
            pl.BlockSpec((FREQS, FREQS), lambda w: (0, 0)),
            pl.BlockSpec((FINE, LENGTH), lambda w: (0, 0)),
            pl.BlockSpec((LENGTH, COARSE * RECV), lambda w: (w, 0)),
        ],
        out_specs=pl.BlockSpec((NPAIR, rows, COARSE * RECV), lambda w: (0, 0, 0)),
        out_shape=jax.ShapeDtypeStruct((NPAIR, rows, COARSE * RECV), bf16),
        scratch_shapes=[pltpu.VMEM((NPAIR, rows, COARSE * RECV), f32)],
        compiler_params=params(),
        cost_estimate=cost(2 * 1024 * 1024 * 4096 * 1.2, 1.5e7),
        name="correlate",
    )(blocks, table, band, fine, recv)


def finish_kernel(x_ref, *refs):
    o_ref = refs[-1]
    total = x_ref[0].astype(f32)
    for p in range(1, NPAIR):
        total = total + x_ref[p].astype(f32)
    total = (total * (1.0 / 128.0)).reshape(PART // 2, FINE, COARSE * RECV)
    for a in range(COARSE):
        o_ref[:, a * FINE:(a + 1) * FINE, :] = total[:, :, a * RECV:(a + 1) * RECV]


def finish(parts, stage, out):
    half = PART // 2
    args, specs, aliases = (parts,), [], {}
    if out is not None:
        args, specs, aliases = (parts, out), [pl.BlockSpec(memory_space=pl.ANY)], {1: 0}
    return pl.pallas_call(
        finish_kernel,
        grid=(2,),
        in_specs=[pl.BlockSpec((NPAIR, half * FINE, COARSE * RECV), lambda i: (0, i, 0))] + specs,
        out_specs=pl.BlockSpec((half, 32, RECV), lambda i: (2 * stage + i, 0, 0)),
        out_shape=jax.ShapeDtypeStruct((32, 32, RECV), f32),
        input_output_aliases=aliases,
        compiler_params=params(),
        cost_estimate=cost(1e6, 3e6),
        name="finish",
    )(*args)


def on_device(raw, taps, source_ids, offsets):
    table, table_t, band, fine, coarse, pick = [jnp.asarray(t) for t in tables()]
    core = lax.axis_index("win") % 2
    swap = [(i, i ^ 1) for i in range(2 * NPAIR)]
    groups = [[2 * p + h for p in range(NPAIR)] for h in range(2)]

    sums, tail = power_and_tail(raw, pick)
    sums = lax.all_to_all(sums, "chan", 0, 0, tiled=True)
    tail = lax.ppermute(tail, "chan", [(j, j + 1) for j in range(NCHAN - 1)])
    own, prior = bands(taps, offsets)
    receivers = decimate_receivers(raw, sums, tail, own, prior)
    receivers = lax.all_to_all(receivers, "chan", 0, 0, tiled=True)
    sources = decimate_sources(
        source_ids, core.reshape(1).astype(jnp.int32), raw, sums, tail, own, prior
    )
    mate = lax.ppermute(sources[1], "win", swap)
    both = jnp.concatenate([sources[0], mate], axis=1)
    both = both.reshape(STAGES, 4, ROWS, OUT)
    stages = [
        lax.all_to_all(
            jnp.broadcast_to(both[s][None], (NCHAN, 4, ROWS, OUT)), "chan", 0, 0, tiled=True
        )
        for s in range(STAGES)
    ]
    spectra = receiver_spectra(receivers, table_t)
    recv = shifted_receivers(spectra, lax.ppermute(spectra, "win", swap), coarse)
    out = None
    for s in range(STAGES):
        parts = correlate(stages[s], table, band, fine, recv)
        parts = lax.all_to_all(parts, "win", 0, 0, tiled=True, axis_index_groups=groups)
        out = finish(parts, s, out)
    return out.reshape(1024, RECV)


def solution(mesh):
    placed = (P("win", None, "chan"), P(), P(), P("win"))
    return jax.shard_map(
        on_device, mesh=mesh, in_specs=placed, out_specs=P("win", "chan"), check_vma=False
    )
```

time: 368 us -> 175 us (0.48)
  waiting for transfers between devices: 214 us -> 48.8 us
  Pallas kernels: 0 us -> 79.4 us
  other arithmetic: 51.1 us -> 2.06 us
  matrix products: 39.5 us -> 0 us
  between operations: 24.8 us -> 0.17 us
  starting transfers between devices: 14.3 us -> 35.9 us
  local copies, waits for them, and re-layouts: 24.2 us -> 8.17 us
    psum x1 -> x0, waiting for transfers between devices: 162 us -> none  [spread(): return lax.psum(jnp.where(mine, x, jnp.zeros_like(x)), axis)]
    pallas_call x0 -> x9, Pallas kernels: none -> 79.4 us  [the longest x2 45.1 us: correlate(): pl.pallas_call(correlate_kernel, grid=(4,), in_specs=[pl.BlockSpec((NCHAN...]
    dot_general x6 -> x0, matrix products: 39.5 us -> none  [the longest x1 30.2 us: contract(): lax.dot_general(modulated, receivers, (((0, 2), (0, 2)), ((), ())), prefe...]
    another operation x2 -> x0, other arithmetic: 33.3 us -> none
    all_to_all x2 -> x6, starting transfers between devices: 14.2 us -> 27.5 us  [the longest x2 11 us: on_device(): lax.all_to_all(parts, 'win', 0, 0, tiled=True, axis_index_groups=groups)]
    unnamed x13 -> x18, local copies, waits for them, and re-layouts: 13.3 us -> 3.32 us
    ppermute x0 -> x3, starting transfers between devices: none -> 8.37 us  [the longest x1 4.03 us: on_device(): tail = lax.ppermute(tail, 'chan', [(j, j + 1) for j in range(NCHAN - 1)])]
    concatenate x2 -> x1, other arithmetic: 5.7 us -> 0.02 us  [on_device(): both = jnp.concatenate([sources[0], mate], axis=1)]
  transfers between devices with their start and end apart: 4 -> 9, of which waited for: 3 -> 5; matrix products, arithmetic and copies ran while one was open for 15% -> 3% of each run, Pallas kernels for 0% -> 37%
where the time goes in v1:
time: 175 us; the launch traced here: 174 us
  Pallas kernels  79.4 us (45%)
  waiting for transfers between devices  48.8 us (28%)
  starting transfers between devices  35.9 us (21%)
  local copies, waits for them, and re-layouts  8.17 us (5%)
  other arithmetic  2.06 us (1%)
    pallas_call x2, Pallas kernels, correlate(): pl.pallas_call(correlate_kernel, grid=(4,), in_specs=[pl.BlockSpec((NCHAN...  45.1 us
    all_to_all x2, waiting for transfers between devices, on_device(): lax.all_to_all(parts, 'win', 0, 0, tiled=True, axis_index_groups=groups)  32.1 us
    all_to_all x2, starting transfers between devices, on_device(): lax.all_to_all(parts, 'win', 0, 0, tiled=True, axis_index_groups=groups)  11 us
    pallas_call x1, Pallas kernels, shifted_receivers(): pl.pallas_call(shift_kernel, grid=(4,), in_specs=[pl.BlockSpec((1, LENGTH...  7.71 us
    pallas_call x1, Pallas kernels, decimate_receivers(): pl.pallas_call(receive_kernel, grid=(NCHAN,), in_specs=[pl.BlockSpec((2,...  7.42 us
    all_to_all x2, waiting for transfers between devices, on_device(): lax.all_to_all(jnp.broadcast_to(both[s][None], (NCHAN, 4, ROWS, OUT)), 'c...  7.15 us
    all_to_all x2, starting transfers between devices, on_device(): lax.all_to_all(jnp.broadcast_to(both[s][None], (NCHAN, 4, ROWS, OUT)), 'c...  7.12 us
    all_to_all x1, waiting for transfers between devices, on_device(): receivers = lax.all_to_all(receivers, 'chan', 0, 0, tiled=True)  6.61 us
  transfers between devices with their start and end apart: 9, of which 5 were waited for; matrix products, arithmetic and copies ran while one was open for 3% of the time, Pallas kernels for 37%

profile of v1, /device:TPU:1, one launch (start us, length us, event | category | flops | bytes accessed | tf_op | source)
XLA Modules:
  0.0 174.5 jit_solution(7193339673909159368)
XLA Ops:
  0.0 0.0 copy-start.8
  0.0 0.0 copy-start.7
  0.0 5.6 %power.1 = (f32[8,2,2048]{2,1,0:T(2,128)}, bf16[2,32,2048]{2,1,0:T(8,128)(2,1)}) custom-call(bf16[2,2048,512]{2,1,0:T(8,128)(2,1)} %x_ref.5, bf16[32,128]{1,0:T(8,128)(2,1)} %constant.40.clone.pick_ref), custom_call_target="tpu_custom_call" | custom-call | flops 400000000 | bytes 5000000 | tf_op jit(solution)/shard_map/power/pallas_call | solution.py:93
  5.6 4.0 %collective-permute-start = (bf16[2,32,2048]{2,1,0:T(8,128)(2,1)}, bf16[2,32,2048]{2,1,0:T(8,128)(2,1)S(1)}, u32[]{:S(2)}, u32[]{:S(2)}) collective-permute-start(bf16[2,32,2048]{2,1,0:T(8,128)(2,1)} %get-tuple-element.8), channel_id=1, source_target_pairs={{0,16},{16,32},{32,48},{48,64},{64,80},{80,96},{96,112},{1,17},{17... | collective-permute-start | bytes 786440 | tf_op jit(solution)/shard_map/ppermute | solution.py:345
  9.6 5.8 %all-to-all-start = ((f32[8,2,2048]{2,1,0:T(2,128)}), f32[8,2,2048]{2,1,0:T(2,128)S(1)}, u32[]{:S(2)}, u32[]{:S(2)}) async-start(f32[8,2,2048]{2,1,0:T(2,128)} %get-tuple-element.7), calls=%async_computation | async-start | bytes 262144 | tf_op jit(solution)/shard_map/all_to_all | solution.py:344
  15.5 0.0 copy-done.8
  15.5 0.1 broadcast_subtract_fusion
  15.6 0.0 copy-done.7
  15.6 0.1 broadcast_add_fusion
  15.7 1.8 %select_reduce_fusion = bf16[2,544,128]{2,1,0:T(8,128)(2,1)S(1)} fusion(f32[32]{0:T(128)S(1)} %convert_element_type.6, s32[2,544,128]{2,1,0:T(8,128)S(1)} %broadcast_add_fusion), kind=kLoop, calls=%fused_computation | loop fusion | flops 13230080 | bytes 835712 | tf_op jit(solution)/shard_map/reduce_sum | solution.py:119
  17.5 0.7 slice.26.own_ref
  18.3 0.6 slice.27.prior_ref
  18.9 2.9 %all-to-all-done.s_ref = f32[8,2,2048]{2,1,0:T(2,128)S(1)} async-done(((f32[8,2,2048]{2,1,0:T(2,128)}), f32[8,2,2048]{2,1,0:T(2,128)S(1)}, u32[]{:S(2)}, u32[]{:S(2)}) %all-to-all-start) | async-done | bytes 131104 | tf_op jit(solution)/shard_map/all_to_all | solution.py:344
  21.8 0.0 copy-start.2
  21.8 0.0 collective-permute-done.t_ref
  21.8 0.7 copy-done.2
  22.4 0.7 copy-done.4
  23.1 7.4 %decimate_receivers.1 = bf16[8,2,256,128]{3,2,1,0:T(8,128)(2,1)} custom-call(bf16[2,2048,512]{2,1,0:T(8,128)(2,1)} %x_ref.5, f32[8,2,2048]{2,1,0:T(2,128)} %copy-done.2, bf16[2,32,2048]{2,1,0:T(8,128)(2,1)} %copy-done.4, bf16[2,512,128]{2,1,0:T(8,128)(2,1)} %slice.26.own_ref, bf16[2,32,128]{2,1,0:T(8,128)(2,1)} %slice.27.prior_ref), custom_call_target="tpu_custom_call" | custom-call | flops 600000000 | bytes 6000000 | tf_op jit(solution)/shard_map/decimate_receivers/pallas_call | solution.py:141
  30.6 3.6 %all-to-all-start.2 = ((bf16[8,2,256,128]{3,2,1,0:T(8,128)(2,1)}), bf16[8,2,256,128]{3,2,1,0:T(8,128)(2,1)S(1)}, u32[]{:S(2)}, u32[]{:S(2)}) async-start(bf16[8,2,256,128]{3,2,1,0:T(8,128)(2,1)} %decimate_receivers.1), calls=%async_computation.2 | async-start | bytes 2097152 | tf_op jit(solution)/shard_map/all_to_all | solution.py:348
  34.1 4.6 %decimate_sources.1 = bf16[2,2,2,8,16,128]{5,4,3,2,1,0:T(8,128)(2,1)} custom-call(s32[4]{0:T(128)} %ids_ref.1, s32[1]{0:T(128)} %bitcast.core_ref, bf16[2,2048,512]{2,1,0:T(8,128)(2,1)} %x_ref.5, f32[8,2,2048]{2,1,0:T(2,128)} %copy-done.2, bf16[2,32,2048]{2,1,0:T(8,128)(2,1)} %copy-done.4, bf16[2,512,128]{2,1,0:T(8,128)(2,1)} %slice.26.own_ref, ...), custom_call_target="tpu_custom_call" | custom-call | flops 150000000 | bytes 2000000 | tf_op jit(solution)/shard_map/decimate_sources/pallas_call | solution.py:172
  38.8 1.0 slice_bitcast_fusion
  39.8 1.7 collective-permute-start.1
  41.5 6.6 %all-to-all-done.2.x_ref = bf16[8,2,256,128]{3,2,1,0:T(8,128)(2,1)S(1)} async-done(((bf16[8,2,256,128]{3,2,1,0:T(8,128)(2,1)}), bf16[8,2,256,128]{3,2,1,0:T(8,128)(2,1)S(1)}, u32[]{:S(2)}, u32[]{:S(2)}) %all-to-all-start.2) | async-done | bytes 1048608 | tf_op jit(solution)/shard_map/all_to_all | solution.py:348
  48.1 1.0 copy-done.1
  49.0 4.2 %receiver_spectra.1.own_ref = bf16[2,1024,256]{2,1,0:T(8,128)(2,1)} custom-call(bf16[8,2,256,128]{3,2,1,0:T(8,128)(2,1)} %copy-done.1, bf16[1024,1024]{1,0:T(8,128)(2,1)} %constant.36.clone.table_ref), custom_call_target="tpu_custom_call" | custom-call | flops 1100000000 | bytes 4000000 | tf_op jit(solution)/shard_map/receiver_spectra/pallas_call | solution.py:206
  53.2 2.7 %collective-permute-start.2 = (bf16[2,1024,256]{2,1,0:T(8,128)(2,1)}, bf16[2,1024,256]{2,1,0:T(8,128)(2,1)S(1)}, u32[]{:S(2)}, u32[]{:S(2)}) collective-permute-start(bf16[2,1024,256]{2,1,0:T(8,128)(2,1)} %receiver_spectra.1.own_ref), channel_id=1, source_target_pairs={{0,1},{1,0},{2,3},{3,2},{4,5},{5,4},{6,7},{7,6},{8,9},{9,8},{10,11... | collective-permute-start | bytes 3145736 | tf_op jit(solution)/shard_map/ppermute | solution.py:362
  55.9 0.0 collective-permute-done.1
  55.9 1.2 broadcast_in_dim.38
  57.1 3.6 %all-to-all-start.4 = ((bf16[8,4,128,128]{3,2,1,0:T(8,128)(2,1)}), bf16[8,4,128,128]{3,2,1,0:T(8,128)(2,1)S(1)}, u32[]{:S(2)}, u32[]{:S(2)}) async-start(bf16[8,4,128,128]{3,2,1,0:T(8,128)(2,1)} %broadcast_in_dim.38), calls=%async_computation.4 | async-start | bytes 2097152 | tf_op jit(solution)/shard_map/all_to_all | solution.py:356
  60.7 0.0 collective-permute-done.2.mate_ref
  60.7 0.0 copy-start.3
  60.7 1.0 copy-done.3
  61.7 7.7 %shifted_receivers.1.recv_ref = bf16[4096,1024]{1,0:T(8,128)(2,1)} custom-call(bf16[2,1024,256]{2,1,0:T(8,128)(2,1)} %receiver_spectra.1.own_ref, bf16[2,1024,256]{2,1,0:T(8,128)(2,1)} %copy-done.3, f32[4,2,512,128]{3,2,1,0:T(8,128)} %constant.39.clone.twiddle_ref), custom_call_target="tpu_custom_call" | custom-call | flops 30000000 | bytes 12000000 | tf_op jit(solution)/shard_map/shifted_receivers/pallas_call | solution.py:236
  69.4 7.2 %all-to-all-done.4.x_ref = bf16[8,4,128,128]{3,2,1,0:T(8,128)(2,1)S(1)} async-done(((bf16[8,4,128,128]{3,2,1,0:T(8,128)(2,1)}), bf16[8,4,128,128]{3,2,1,0:T(8,128)(2,1)S(1)}, u32[]{:S(2)}, u32[]{:S(2)}) %all-to-all-start.4) | async-done | bytes 1048608 | tf_op jit(solution)/shard_map/all_to_all | solution.py:356
  76.5 1.3 broadcast_in_dim.36
  77.8 3.6 %all-to-all-start.1 = ((bf16[8,4,128,128]{3,2,1,0:T(8,128)(2,1)}), bf16[8,4,128,128]{3,2,1,0:T(8,128)(2,1)S(1)}, u32[]{:S(2)}, u32[]{:S(2)}) async-start(bf16[8,4,128,128]{3,2,1,0:T(8,128)(2,1)} %broadcast_in_dim.36), calls=%async_computation.1 | async-start | bytes 2097152 | tf_op jit(solution)/shard_map/all_to_all | solution.py:356
  81.4 0.0 copy-done.5
  81.4 22.5 %correlate.3 = bf16[8,128,1024]{2,1,0:T(8,128)(2,1)} custom-call(bf16[8,4,128,128]{3,2,1,0:T(8,128)(2,1)} %copy-done.5, bf16[1024,1024]{1,0:T(8,128)(2,1)} %constant.35.clone.table_ref, bf16[512,512]{1,0:T(8,128)(2,1)} %constant.37.clone.band_ref, f32[8,1024]{1,0:T(8,128)} %constant.38.clone.fine_ref, bf16[4096,1024]{1,0:T(8,128)(2,1)} %shifted_receivers.1.recv_ref), custom_call_target="tpu_custom_call" | custom-call | flops 10307921920 | bytes 15000000 | tf_op jit(solution)/shard_map/correlate/pallas_call | solution.py:290
  103.9 0.0 all-to-all-done.1.x_ref
  103.9 6.7 %all-to-all-start.5 = ((bf16[8,128,1024]{2,1,0:T(8,128)(2,1)}), bf16[8,128,1024]{2,1,0:T(8,128)(2,1)S(1)}, u32[]{:S(2)}, u32[]{:S(2)}) async-start(bf16[8,128,1024]{2,1,0:T(8,128)(2,1)} %correlate.3), calls=%async_computation.5 | async-start | bytes 4194304 | tf_op jit(solution)/shard_map/all_to_all | solution.py:366
  110.6 0.0 copy-done.6
  110.6 22.5 %correlate.2 = bf16[8,128,1024]{2,1,0:T(8,128)(2,1)} custom-call(bf16[8,4,128,128]{3,2,1,0:T(8,128)(2,1)} %copy-done.6, bf16[1024,1024]{1,0:T(8,128)(2,1)} %constant.35.clone.table_ref, bf16[512,512]{1,0:T(8,128)(2,1)} %constant.37.clone.band_ref, f32[8,1024]{1,0:T(8,128)} %constant.38.clone.fine_ref, bf16[4096,1024]{1,0:T(8,128)(2,1)} %shifted_receivers.1.recv_ref), custom_call_target="tpu_custom_call" | custom-call | flops 10307921920 | bytes 15000000 | tf_op jit(solution)/shard_map/correlate/pallas_call | solution.py:290
  133.2 6.0 %all-to-all-done.5.x_ref = bf16[8,128,1024]{2,1,0:T(8,128)(2,1)S(1)} async-done(((bf16[8,128,1024]{2,1,0:T(8,128)(2,1)}), bf16[8,128,1024]{2,1,0:T(8,128)(2,1)S(1)}, u32[]{:S(2)}, u32[]{:S(2)}) %all-to-all-start.5) | async-done | bytes 2097184 | tf_op jit(solution)/shard_map/all_to_all | solution.py:366
  139.1 4.4 %all-to-all-start.3 = ((bf16[8,128,1024]{2,1,0:T(8,128)(2,1)}), bf16[8,128,1024]{2,1,0:T(8,128)(2,1)}, u32[]{:S(2)}, u32[]{:S(2)}) async-start(bf16[8,128,1024]{2,1,0:T(8,128)(2,1)} %correlate.2), calls=%async_computation.3 | async-start | bytes 4194304 | tf_op jit(solution)/shard_map/all_to_all | solution.py:366
  143.5 0.0 copy-done
  143.5 2.4 %finish.2.refs_0_ = f32[32,32,256]{2,1,0:T(8,128)} custom-call(bf16[8,128,1024]{2,1,0:T(8,128)(2,1)} %copy-done), custom_call_target="tpu_custom_call" | custom-call | flops 1000000 | bytes 3000000 | tf_op jit(solution)/shard_map/finish/pallas_call | solution.py:324
  145.9 26.1 %all-to-all-done.3.x_ref = bf16[8,128,1024]{2,1,0:T(8,128)(2,1)} async-done(((bf16[8,128,1024]{2,1,0:T(8,128)(2,1)}), bf16[8,128,1024]{2,1,0:T(8,128)(2,1)}, u32[]{:S(2)}, u32[]{:S(2)}) %all-to-all-start.3) | async-done | bytes 2097184 | tf_op jit(solution)/shard_map/all_to_all | solution.py:366
  172.1 2.4 %finish.3 = f32[32,32,256]{2,1,0:T(8,128)} custom-call(bf16[8,128,1024]{2,1,0:T(8,128)(2,1)} %all-to-all-done.3.x_ref, f32[32,32,256]{2,1,0:T(8,128)} %finish.2.refs_0_), custom_call_target="tpu_custom_call", output_to_operand_aliasing={{}: (1, {})} | custom-call | flops 1000000 | bytes 3000000 | tf_op jit(solution)/shard_map/finish/pallas_call | solution.py:324
  (9 shorter events, 0.0 us)
Async XLA Ops:
  0.0 15.5 %copy-start.8 = (bf16[32]{0:T(256)(128)(2,1)S(1)}, bf16[32]{0:T(256)(128)(2,1)}, u32[]{:S(2)}) copy-start(bf16[32]{0:T(256)(128)(2,1)} %param.11) | copy-start | bytes 196
  0.0 15.6 %copy-start.7 = (s32[2]{0:T(128)S(1)}, s32[2]{0:T(128)}, u32[]{:S(2)}) copy-start(s32[2]{0:T(128)} %param.13) | copy-start | bytes 28
  5.6 16.2 %collective-permute-start = (bf16[2,32,2048]{2,1,0:T(8,128)(2,1)}, bf16[2,32,2048]{2,1,0:T(8,128)(2,1)S(1)}, u32[]{:S(2)}, u32[]{:S(2)}) collective-permute-start(bf16[2,32,2048]{2,1,0:T(8,128)(2,1)} %get-tuple-element.8), channel_id=1, source_target_pairs={{0,16},{16,32},{32,48},{48,64},{64,80},{80,96},{96,112},{1,17},{17... | collective-permute-start | bytes 786440 | tf_op jit(solution)/shard_map/ppermute | solution.py:345
  9.6 12.1 %all-to-all-start = ((f32[8,2,2048]{2,1,0:T(2,128)}), f32[8,2,2048]{2,1,0:T(2,128)S(1)}, u32[]{:S(2)}, u32[]{:S(2)}) async-start(f32[8,2,2048]{2,1,0:T(2,128)} %get-tuple-element.7), calls=%async_computation | async-start | bytes 262144 | tf_op jit(solution)/shard_map/all_to_all | solution.py:344
  21.8 0.7 copy-start.2
  22.4 0.7 copy-start.4
  30.6 17.5 %all-to-all-start.2 = ((bf16[8,2,256,128]{3,2,1,0:T(8,128)(2,1)}), bf16[8,2,256,128]{3,2,1,0:T(8,128)(2,1)S(1)}, u32[]{:S(2)}, u32[]{:S(2)}) async-start(bf16[8,2,256,128]{3,2,1,0:T(8,128)(2,1)} %decimate_receivers.1), calls=%async_computation.2 | async-start | bytes 2097152 | tf_op jit(solution)/shard_map/all_to_all | solution.py:348
  39.8 16.1 %collective-permute-start.1 = (bf16[2,2,8,16,128]{4,3,2,1,0:T(8,128)(2,1)S(1)}, bf16[2,2,8,16,128]{4,3,2,1,0:T(8,128)(2,1)S(1)}, u32[]{:S(2)}, u32[]{:S(2)}) collective-permute-start(bf16[2,2,8,16,128]{4,3,2,1,0:T(8,128)(2,1)S(1)} %get-tuple-element.11), channel_id=1, source_target_pairs={{0,1},{1,0},{2,3},{3,2},{4,5},{5,4},{6,7},{7,6},{8,9},{9,8},{10,11... | collective-permute-start | bytes 393224 | tf_op jit(solution)/shard_map/ppermute | solution.py:352
  48.1 1.0 copy-start.1
  53.2 7.5 %collective-permute-start.2 = (bf16[2,1024,256]{2,1,0:T(8,128)(2,1)}, bf16[2,1024,256]{2,1,0:T(8,128)(2,1)S(1)}, u32[]{:S(2)}, u32[]{:S(2)}) collective-permute-start(bf16[2,1024,256]{2,1,0:T(8,128)(2,1)} %receiver_spectra.1.own_ref), channel_id=1, source_target_pairs={{0,1},{1,0},{2,3},{3,2},{4,5},{5,4},{6,7},{7,6},{8,9},{9,8},{10,11... | collective-permute-start | bytes 3145736 | tf_op jit(solution)/shard_map/ppermute | solution.py:362
  57.1 19.4 %all-to-all-start.4 = ((bf16[8,4,128,128]{3,2,1,0:T(8,128)(2,1)}), bf16[8,4,128,128]{3,2,1,0:T(8,128)(2,1)S(1)}, u32[]{:S(2)}, u32[]{:S(2)}) async-start(bf16[8,4,128,128]{3,2,1,0:T(8,128)(2,1)} %broadcast_in_dim.38), calls=%async_computation.4 | async-start | bytes 2097152 | tf_op jit(solution)/shard_map/all_to_all | solution.py:356
  60.7 1.0 copy-start.3
  76.5 4.9 %copy-start.5 = (bf16[8,4,128,128]{3,2,1,0:T(8,128)(2,1)}, bf16[8,4,128,128]{3,2,1,0:T(8,128)(2,1)S(1)}, u32[]{:S(2)}) copy-start(bf16[8,4,128,128]{3,2,1,0:T(8,128)(2,1)S(1)} %all-to-all-done.4.x_ref) | copy-start | bytes 3145732
  77.8 26.1 %all-to-all-start.1 = ((bf16[8,4,128,128]{3,2,1,0:T(8,128)(2,1)}), bf16[8,4,128,128]{3,2,1,0:T(8,128)(2,1)S(1)}, u32[]{:S(2)}, u32[]{:S(2)}) async-start(bf16[8,4,128,128]{3,2,1,0:T(8,128)(2,1)} %broadcast_in_dim.36), calls=%async_computation.1 | async-start | bytes 2097152 | tf_op jit(solution)/shard_map/all_to_all | solution.py:356
  103.9 6.7 %copy-start.6 = (bf16[8,4,128,128]{3,2,1,0:T(8,128)(2,1)}, bf16[8,4,128,128]{3,2,1,0:T(8,128)(2,1)S(1)}, u32[]{:S(2)}) copy-start(bf16[8,4,128,128]{3,2,1,0:T(8,128)(2,1)S(1)} %all-to-all-done.1.x_ref) | copy-start | bytes 3145732
  103.9 35.2 %all-to-all-start.5 = ((bf16[8,128,1024]{2,1,0:T(8,128)(2,1)}), bf16[8,128,1024]{2,1,0:T(8,128)(2,1)S(1)}, u32[]{:S(2)}, u32[]{:S(2)}) async-start(bf16[8,128,1024]{2,1,0:T(8,128)(2,1)} %correlate.3), calls=%async_computation.5 | async-start | bytes 4194304 | tf_op jit(solution)/shard_map/all_to_all | solution.py:366
  139.1 4.4 %copy-start = (bf16[8,128,1024]{2,1,0:T(8,128)(2,1)}, bf16[8,128,1024]{2,1,0:T(8,128)(2,1)S(1)}, u32[]{:S(2)}) copy-start(bf16[8,128,1024]{2,1,0:T(8,128)(2,1)S(1)} %all-to-all-done.5.x_ref) | copy-start | bytes 6291460
  139.1 32.9 %all-to-all-start.3 = ((bf16[8,128,1024]{2,1,0:T(8,128)(2,1)}), bf16[8,128,1024]{2,1,0:T(8,128)(2,1)}, u32[]{:S(2)}, u32[]{:S(2)}) async-start(bf16[8,128,1024]{2,1,0:T(8,128)(2,1)} %correlate.2), calls=%async_computation.3 | async-start | bytes 4194304 | tf_op jit(solution)/shard_map/all_to_all | solution.py:366
